TPU v7x, 256 devices: a whole 4x4x8 slice. The times are simulated.
256 devices in a mesh: seq: 16 (over y, z_lo, core), head: 16 (over x, z_hi).
Axes of the slice: x: 4, y: 4, z: 8 (z_hi: 4, z_lo: 2; z = z_hi * 2 + z_lo), core: 2. Of those that a mesh axis runs over, the one named last changes fastest.
Arguments:
- span_x: bfloat16 [4096, 5120], P('seq', 'head'), may hold values from -6 to 6
- cand_x: bfloat16 [16, 128, 5120], P('seq', None, 'head'), may hold values from -6 to 6
- cand_len: int32 [16], P('seq'), may hold values from 32 to 128, as said below
- offset: int32 [1], replicated, may hold values from 7936 to 8192
- norm_gain: float32 [5120], replicated, may hold values from 0.1 to 1.9
- wq: bfloat16 [5120, 8192], P(None, 'head'), may hold values from -0.078125 to 0.078125
- wk: bfloat16 [5120, 1024], P(None, 'head'), may hold values from -0.078125 to 0.078125
- wv: bfloat16 [5120, 1024], P(None, 'head'), may hold values from -0.078125 to 0.078125
- q_gain: float32 [128], replicated, may hold values from 1 to 3
- k_gain: float32 [128], replicated, may hold values from 1 to 3
- wo: bfloat16 [8192, 5120], P('head'), may hold values from -0.25 to 0.25
- cache_k: bfloat16 [8192, 1024], P('seq', 'head'), may hold values from -70 to 70
- cache_v: bfloat16 [8192, 1024], P('seq', 'head'), may hold values from -6 to 6
Outputs:
- span_out: bfloat16 [4096, 5120], P('seq', 'head')
- cand_out: bfloat16 [16, 128, 5120], P('seq', None, 'head')
Inputs may be any that keep to these rules, and one draw needn't show every extreme that they name: `cand_len`: each candidate's real tokens; its remaining rows are padding; some candidate has all 128. Cache slots at or after offset hold no source token and are never visible.
All inputs are finite; a program needn't handle non-finite values.
Results may differ from a plain program's by a relative error of at most 0.024.
The roundings to bfloat16 on the way count: a program that leaves them out, or rounds other values in their place, can miss the bound.
Values may be sent and summed in bfloat16 or wider, within the bound.
No kernel may reach another device: no remote copies, remote signals or barrier semaphores. Data moves between devices by JAX's collectives and lax.ppermute only.
A program may use at most 128 MiB of HBM per device.

v0:
```python
import math

import jax
import jax.numpy as jnp
from jax import lax
from jax.sharding import PartitionSpec as P

epsilon = 1e-06
rope_base = 1000000.0


def partner_2(block, axis, stride):
    count = lax.axis_size(axis)
    route = []
    for low in range(count):
        high = low | 1 << stride
        if high != low and high < count:
            route += [(low, high), (high, low)]
    return lax.ppermute(block, axis, route)


def rms_scale(values, gain):
    mean_square = jnp.mean(values * values, axis=-1, keepdims=True)
    return values * lax.rsqrt(mean_square + epsilon) * gain


def rotate(values, positions):
    head_width = values.shape[-1]
    half_width = head_width // 2
    frequency = rope_base ** (-(jnp.arange(half_width, dtype=jnp.float32) * 2.0 / head_width))
    angles = positions.astype(jnp.float32)[:, None] * frequency[None, :]
    cosine = jnp.cos(angles)[:, None, :]
    sine_part = jnp.sin(angles)[:, None, :]
    front_half = values[..., :half_width]
    back_half = values[..., half_width:]
    return jnp.concatenate(
        [front_half * cosine - back_half * sine_part, back_half * cosine + front_half * sine_part],
        axis=-1,
    )


def join_halves(mine, other, parity):
    return jnp.where(
        parity == 0,
        jnp.concatenate([mine, other], axis=-1),
        jnp.concatenate([other, mine], axis=-1),
    )


def finish_keys(raw_keys, k_gain, positions):
    normed_keys = rms_scale(raw_keys.astype(jnp.float32)[:, None, :], k_gain)
    return rotate(normed_keys, positions)[:, 0, :].astype(jnp.bfloat16)


def update(state, scores, visible, values):
    running_top, totals, accum = state
    masked = jnp.where(visible, scores, -1e30)
    new_top = jnp.maximum(running_top, jnp.max(masked, axis=-1))
    weights = jnp.where(visible, jnp.exp(masked - new_top[..., None]), 0.0)
    factor = jnp.exp(running_top - new_top)
    totals = totals * factor + jnp.sum(weights, axis=-1)
    accum = accum * factor[..., None] + jnp.einsum(
        "hqk,kd->hqd", weights.astype(jnp.bfloat16), values, preferred_element_type=jnp.float32
    )
    return (new_top, totals, accum)


def attend_source(queries, limits, source, cache_len, span_len, span_start, score_scale):
    head_size = queries.shape[2]
    block_rows = cache_len + span_len
    blocks = source.reshape(-1, block_rows, 2 * head_size)
    query_rows = queries.shape[0]
    heads_here = queries.shape[1]
    initial = (
        jnp.full((heads_here, query_rows), -1e30, jnp.float32),
        jnp.zeros((heads_here, query_rows), jnp.float32),
        jnp.zeros((heads_here, query_rows, head_size), jnp.float32),
    )
    key_local = jnp.arange(block_rows, dtype=jnp.int32)
    is_cache = key_local < cache_len

    def fold_block(state, item):
        block_idx, block_data = item
        scores = (
            jnp.einsum(
                "qhd,kd->hqk",
                queries,
                block_data[:, :head_size],
                preferred_element_type=jnp.float32,
            )
            * score_scale
        )
        cache_seen = is_cache & (block_idx * cache_len + key_local < span_start)
        span_seen = (~is_cache)[None, :] & (
            (block_idx * span_len + key_local - cache_len)[None, :] <= limits[:, None]
        )
        visible = (cache_seen[None, :] | span_seen)[None]
        return (update(state, scores, visible, block_data[:, head_size:]), None)

    state, _ = lax.scan(fold_block, initial, (jnp.arange(blocks.shape[0], dtype=jnp.int32), blocks))
    return state


def attend_own(state, queries, own_keys, own_values, cand_width, score_scale):
    scores = (
        jnp.einsum("qhd,kd->hqk", queries, own_keys, preferred_element_type=jnp.float32)
        * score_scale
    )
    row_ids = jnp.arange(queries.shape[0], dtype=jnp.int32)
    same_cand = row_ids[:, None] // cand_width == row_ids[None, :] // cand_width
    visible = (same_cand & (row_ids[None, :] <= row_ids[:, None]))[None]
    return update(state, scores, visible, own_values)


def finish(state):
    attended = state[2] / state[1][..., None]
    heads_here, query_rows, head_size = attended.shape
    return (
        attended.transpose(1, 0, 2).reshape(query_rows, heads_here * head_size).astype(jnp.bfloat16)
    )


def per_device(
    span_x, cand_x, cand_len, offset, norm_gain, wq, wk, wv, q_gain, k_gain, wo, cache_k, cache_v
):
    seq_count = lax.axis_size("seq")
    seq_pos = lax.axis_index("seq")
    parity = lax.axis_index("head") % 2
    head_size = q_gain.shape[0]
    half_width = head_size // 2
    score_scale = 1.0 / math.sqrt(head_size)
    span_len = span_x.shape[0]
    cand_count = cand_x.shape[0]
    cand_width = cand_x.shape[1]
    cand_rows = cand_count * cand_width
    cache_len = cache_k.shape[0]
    span_start = offset[0]
    span_full, cand_full = (
        lax.all_gather(span_x, "head", axis=1, tiled=True),
        lax.all_gather(cand_x.reshape(cand_rows, cand_x.shape[2]), "head", axis=1, tiled=True),
    )
    all_rows = jnp.concatenate([span_full, cand_full], axis=0)
    span_positions = span_start + seq_pos * span_len + jnp.arange(span_len, dtype=jnp.int32)
    cand_positions = (
        span_start
        + span_len * seq_count
        + jnp.tile(jnp.arange(cand_width, dtype=jnp.int32), cand_count)
    )
    positions = jnp.concatenate([span_positions, cand_positions])
    normed = rms_scale(all_rows.astype(jnp.float32), norm_gain).astype(jnp.bfloat16)
    queries = jnp.dot(normed, wq, preferred_element_type=jnp.float32)
    queries = queries.reshape(queries.shape[0], wq.shape[1] // head_size, head_size)
    queries = rotate(rms_scale(queries, q_gain), positions).astype(jnp.bfloat16)
    key_half = jnp.dot(normed, wk, preferred_element_type=jnp.float32).astype(jnp.bfloat16)
    value_half = jnp.dot(normed, wv, preferred_element_type=jnp.float32).astype(jnp.bfloat16)
    new_half = jnp.concatenate([key_half, value_half], axis=1)
    cache_half = jnp.concatenate([cache_k, cache_v], axis=1)
    local_half = jnp.concatenate([cache_half, new_half], axis=0)
    partner = partner_2(local_half, "head", 0)
    key_all = join_halves(local_half[:, :half_width], partner[:, :half_width], parity)
    value_all = join_halves(local_half[:, half_width:], partner[:, half_width:], parity)
    new_keys = finish_keys(key_all[cache_len:], k_gain, positions)
    own_values = value_all[cache_len + span_len :]
    source_keys = jnp.concatenate([key_all[:cache_len], new_keys[:span_len]], axis=0)
    block_data = jnp.concatenate([source_keys, value_all[: cache_len + span_len]], axis=1)
    source = lax.all_gather(block_data, "seq", axis=0, tiled=True)
    own_keys = new_keys[span_len:]
    span_limits = seq_pos * span_len + jnp.arange(span_len, dtype=jnp.int32)
    cand_limits = jnp.full((cand_rows,), span_len * seq_count, jnp.int32)
    cand_valid = (jnp.arange(cand_width, dtype=jnp.int32)[None, :] < cand_len[:, None]).reshape(
        cand_rows, 1
    )
    limits = jnp.concatenate([span_limits, cand_limits])
    state = attend_source(queries, limits, source, cache_len, span_len, span_start, score_scale)
    cand_state = attend_own(
        tuple((member[:, span_len:] for member in state)),
        queries[span_len:],
        own_keys,
        own_values,
        cand_width,
        score_scale,
    )
    merged = tuple(
        (
            jnp.concatenate([member[:, :span_len], own_part], axis=1)
            for member, own_part in zip(state, cand_state)
        )
    )
    terms = jnp.dot(finish(merged), wo, preferred_element_type=jnp.float32)
    summed = lax.psum_scatter(
        terms.astype(jnp.bfloat16), "head", scatter_dimension=1, tiled=True
    ).astype(jnp.float32)
    span_sum = summed[:span_len]
    cand_sum = summed[span_len:]
    span_out = span_sum.astype(jnp.bfloat16)
    cand_out = (
        jnp.where(cand_valid, cand_sum, 0.0)
        .astype(jnp.bfloat16)
        .reshape(cand_count, cand_width, cand_sum.shape[1])
    )
    return (span_out, cand_out)


def solution(mesh):
    in_specs = (
        P("seq", "head"),
        P("seq", None, "head"),
        P("seq"),
        P(),
        P(),
        P(None, "head"),
        P(None, "head"),
        P(None, "head"),
        P(),
        P(),
        P("head", None),
        P("seq", "head"),
        P("seq", "head"),
    )
    out_specs = (P("seq", "head"), P("seq", None, "head"))
    return jax.shard_map(
        per_device, mesh=mesh, in_specs=in_specs, out_specs=out_specs, check_vma=False
    )
```

profile of v0, /device:TPU:31, one launch (start us, length us, event | category | flops | bytes accessed | tf_op | source)
XLA Modules:
  0.0 522.3 jit_solution(973339893087675213)
XLA Ops:
  9.4 55.8 %all-gather.9.cloned.1.call-done = bf16[1,128,5120]{1,2,0:T(8,128)(2,1)} async-done(((bf16[1,128,320]{1,2,0:T(8,128)(2,1)}), bf16[1,128,5120]{1,2,0:T(8,128)(2,1)}) %all-gather.9.cloned.1.call-update) | async-done | bytes 1310736 | tf_op jit(solution)/shard_map/all_gather | solution.py:140
  65.3 65.9 %all-gather.5.cloned.1.call-done = bf16[256,5120]{0,1:T(8,128)(2,1)} async-done(((bf16[256,320]{0,1:T(8,128)(2,1)}), bf16[256,5120]{0,1:T(8,128)(2,1)}) %all-gather.5.cloned.1.call-update) | async-done | bytes 2621456 | tf_op jit(solution)/shard_map/all_gather | solution.py:139
  131.2 3.3 fusion.23
  134.5 2.7 fusion.25
  139.1 2.1 collective-permute-start
  141.2 9.8 %collective-permute-done = bf16[896,128]{0,1:T(8,128)(2,1)S(1)} collective-permute-done((bf16[896,128]{0,1:T(8,128)(2,1)S(1)}, bf16[896,128]{0,1:T(8,128)(2,1)S(1)}, u32[]{:S(2)}, u32[]{:S(2)}) %collective-permute-start) | collective-permute-done | bytes 229408 | tf_op jit(solution)/shard_map/ppermute | solution.py:19
  154.4 5.9 %fusion.61 = f32[384,512]{1,0:T(8,128)S(1)} fusion(bf16[384,5120]{0,1:T(8,128)(2,1)} %copy-done.2, bf16[5120,512]{1,0:T(8,128)(2,1)} %param.20), kind=kOutput, calls=%fused_computation.116 | convolution fusion | flops 2013265920 | bytes 9961472 | tf_op jit(solution)/shard_map/dot_general | solution.py:151
  164.1 33.1 %all-gather.7.cloned.1.call-done = bf16[12288,256]{0,1:T(8,128)(2,1)} async-done(((bf16[768,256]{0,1:T(8,128)(2,1)}), bf16[12288,256]{0,1:T(8,128)(2,1)}) %all-gather.7.cloned.1.call-update) | async-done | bytes 6291472 | tf_op jit(solution)/shard_map/all_gather | solution.py:166
  197.2 8.6 %copy.51 = bf16[12288,256]{1,0:T(8,128)(2,1)} copy(bf16[12288,256]{0,1:T(8,128)(2,1)} %all-gather.7.cloned.1.call-done) | data formatting | bytes 12582912
  205.8 206.3 %while.18 = (s32[]{:T(128)}, f32[4,384]{1,0:T(4,128)S(1)}, f32[4,384]{1,0:T(4,128)S(1)}, f32[4,384,128]{2,1,0:T(8,128)S(1)}, s32[16]{0:T(128)S(1)}, /*index=5*/s...) while((s32[]{:T(128)}, f32[4,384]{1,0:T(4,128)S(1)}, ...), condition=%wide.region_6.7_spmd.clone.clone, body=%wide.region_3.6_spmd.clone.clone.sunk | while | flops 620803584 | bytes 37464792 | solution.py:100
  210.2 3.1 fusion.84
  213.3 3.6 fusion.85
  217.0 1.7 fusion.87
  223.1 3.1 fusion.84
  226.2 3.6 fusion.85
  229.9 1.7 fusion.87
  236.0 3.1 fusion.84
  239.0 3.6 fusion.85
  248.9 3.1 fusion.84
  251.9 3.6 fusion.85
  255.7 1.7 fusion.87
  261.8 3.1 fusion.84
  264.8 3.6 fusion.85
  274.7 3.1 fusion.84
  277.7 3.6 fusion.85
  281.5 1.7 fusion.87
  287.6 3.1 fusion.84
  290.6 3.6 fusion.85
  300.4 3.1 fusion.84
  303.5 3.6 fusion.85
  313.3 3.1 fusion.84
  316.4 3.6 fusion.85
  326.2 3.1 fusion.84
  329.3 3.6 fusion.85
  339.1 3.1 fusion.84
  342.2 3.6 fusion.85
  352.0 3.1 fusion.84
  355.1 3.6 fusion.85
  364.9 3.1 fusion.84
  368.0 3.6 fusion.85
  377.8 3.1 fusion.84
  380.9 3.6 fusion.85
  390.7 3.1 fusion.84
  393.8 3.6 fusion.85
  403.6 3.1 fusion.84
  406.7 3.6 fusion.85
  413.0 7.3 %convolution_convert_fusion = bf16[384,5120]{0,1:T(8,128)(2,1)} fusion(bf16[384,512]{0,1:T(8,128)(2,1)S(1)} %bitcast.92, bf16[512,5120]{1,0:T(8,128)(2,1)} %param.25), kind=kOutput, calls=%fused_computation.36 | convolution fusion | flops 2015232000 | bytes 9568256 | tf_op jit(solution)/shard_map/dot_general | solution.py:189
  421.0 91.7 %reduce-scatter.2.cloned.1.call-done = bf16[384,320]{0,1:T(8,128)(2,1)} async-done(((bf16[384,5120]{0,1:T(8,128)(2,1)}), bf16[384,320]{0,1:T(8,128)(2,1)}) %reduce-scatter.2.cloned.1.call-update) | async-done | bytes 245776 | tf_op jit(solution)/shard_map/reduce_scatter | solution.py:190
  (265 shorter events, 84.8 us)
Async XLA Ops:
  7.2 130.0 %copy-start = (bf16[5120,64]{0,1:T(8,128)(2,1)S(1)}, bf16[5120,64]{0,1:T(8,128)(2,1)}, u32[]{:S(2)}) copy-start(bf16[5120,64]{0,1:T(8,128)(2,1)} %param.22) | copy-start | bytes 1966084
  7.2 58.1 %all-gather.9.cloned.1.call-start = ((), (), s32[]{:S(2)}) async-start(), calls=%async_computation.4 | async-start | bytes 1392640 | tf_op jit(solution)/shard_map/all_gather | solution.py:140
  7.9 123.3 %all-gather.5.cloned.1.call-start = ((), (), s32[]{:S(2)}) async-start(), calls=%async_computation.1 | async-start | bytes 2785280 | tf_op jit(solution)/shard_map/all_gather | solution.py:139
  8.7 188.6 %all-gather.7.cloned.1.call-start = ((), (), s32[]{:S(2)}) async-start(), calls=%async_computation.2 | async-start | bytes 6684672 | tf_op jit(solution)/shard_map/all_gather | solution.py:166
  65.3 69.2 %copy-start.4 = (bf16[1,128,5120]{1,2,0:T(8,128)(2,1)S(1)}, bf16[1,128,5120]{1,2,0:T(8,128)(2,1)}, u32[]{:S(2)}) copy-start(bf16[1,128,5120]{1,2,0:T(8,128)(2,1)} %all-gather.9.cloned.1.call-done) | copy-start | bytes 3932164
  131.2 3.3 copy-start.3
  134.5 3.4 copy-start.5
  137.2 1.9 copy-start.2
  137.2 1.5 copy-start.7
  137.2 1.5 copy-start.8
  137.9 13.3 %copy-start.9 = (f32[128]{0:T(128)S(1)}, f32[128]{0:T(128)}, u32[]{:S(2)}) copy-start(f32[128]{0:T(128)} %param.24) | copy-start | bytes 1540
  139.1 11.9 %collective-permute-start = (bf16[896,128]{0,1:T(8,128)(2,1)S(1)}, bf16[896,128]{0,1:T(8,128)(2,1)S(1)}, u32[]{:S(2)}, u32[]{:S(2)}) collective-permute-start(bf16[896,128]{0,1:T(8,128)(2,1)S(1)} %maximum_maximum_fusion), channel_id=1, source_target_pairs={{0,1},{1,0},{2,3},{3,2},{4,5},{5,4},{6,7},{7,6},{8,9},{9,8},{10,11... | collective-permute-start | bytes 688136 | tf_op jit(solution)/shard_map/ppermute | solution.py:19
  151.8 0.9 copy-start.6
  152.7 360.0 %reduce-scatter.2.cloned.1.call-start = ((), (), s32[]{:S(2)}) async-start(), calls=%async_computation.3 | async-start | bytes 4177920 | tf_op jit(solution)/shard_map/reduce_scatter | solution.py:190
  154.4 6.8 %copy-start.10 = (f32[128]{0:T(128)S(1)}, f32[128]{0:T(128)}, u32[]{:S(2)}) copy-start(f32[128]{0:T(128)} %param.23) | copy-start | bytes 1540
  213.3 3.8 copy-start.1
  226.1 3.8 copy-start.1
  239.0 3.8 copy-start.1
  251.9 3.8 copy-start.1
  264.8 3.8 copy-start.1
  277.7 3.8 copy-start.1
  290.6 3.8 copy-start.1
  303.5 3.8 copy-start.1
  316.4 3.8 copy-start.1
  329.3 3.8 copy-start.1
  342.2 3.8 copy-start.1
  355.1 3.8 copy-start.1
  368.0 3.8 copy-start.1
  380.9 3.8 copy-start.1
  393.8 3.8 copy-start.1
  406.6 3.8 copy-start.1
Sparse Core Ops, SparseCore 0:
  10.5 54.7 all-gather.8
  67.7 63.3 all-gather.4
  152.8 44.4 all-gather.6
  420.4 92.2 reduce-scatter.1
where the time goes:
time: 527 us; the launch traced here: 522 us
  waiting for transfers between devices  258 us (49%)
  other arithmetic  94.6 us (18%)
  matrix products  91.8 us (17%)
  local copies, waits for them, and re-layouts  38.6 us (7%)
  loops' own time  21.7 us (4%)
  between operations  15.5 us (3%)
    reduce_scatter x1, waiting for transfers between devices, per_device(): lax.psum_scatter(terms.astype(jnp.bfloat16), 'head', scatter_dimension=1,...  91.7 us
    all_gather x1, waiting for transfers between devices, per_device(): lax.all_gather(span_x, 'head', axis=1, tiled=True)  65.9 us
    reduce_sum x17, other arithmetic, update(): totals = totals * factor + jnp.sum(weights, axis=-1)  58.4 us
    all_gather x1, waiting for transfers between devices, per_device(): lax.all_gather(cand_x.reshape(cand_rows, cand_x.shape[2]), 'head', axis=1...  55.8 us
    dot_general x16, matrix products, fold_block(): jnp.einsum('qhd,kd->hqk', queries, block_data[:, :head_size], preferred_e...  48.9 us
    all_gather x1, waiting for transfers between devices, per_device(): source = lax.all_gather(block_data, 'seq', axis=0, tiled=True)  33.1 us
    dot_general x17, matrix products, update(): jnp.einsum('hqk,kd->hqd', weights.astype(jnp.bfloat16), values, preferred...  27.3 us
    another operation x1, loops' own time, attend_source(): lax.scan(fold_block, initial, (jnp.arange(blocks.shape[0], dtype=jnp.int3...  21.7 us
  transfers between devices with their start and end apart: 5, of which 5 were waited for; matrix products, arithmetic and copies ran while one was open for 2% of the time, Pallas kernels for 0%

commit v1 on v0

v1 whole, which is shorter than its diff:
```python
import functools
import math

import jax
import jax.numpy as jnp
from jax import lax
from jax.experimental import pallas as pl
from jax.experimental.pallas import tpu as pltpu
from jax.sharding import PartitionSpec as P

epsilon = 1e-06
rope_base = 1000000.0
NX = 4
NZ = 4
HEADS = 4
HD = 128
SPAN_ROWS = 256
CAND_ROWS = 128
ROWS = SPAN_ROWS + CAND_ROWS
LOG2E = 1.4426950408889634
VMEM = 56 * 1024 * 1024


def move_x(block, step):
    route = []
    for x in range(NX):
        for z in range(NZ):
            route.append((x * NZ + z, (x + step) % NX * NZ + z))
    return lax.ppermute(block, "head", route)


def move_z(block, step):
    route = []
    for x in range(NX):
        for z in range(NZ):
            route.append((x * NZ + z, x * NZ + (z + step) % NZ))
    return lax.ppermute(block, "head", route)


def swap_pair(block):
    return lax.ppermute(block, "head", [(h, h ^ 1) for h in range(NX * NZ)])


def project_kernel(place, *refs):
    blocks = refs[: NX * NZ]
    gain, wq, wkv_t, q_gain, cosine, sine, q_out, kv_out, normed = refs[NX * NZ :]
    width = blocks[0].shape[0]
    features = width * NX * NZ
    total = jnp.zeros((1, ROWS), jnp.float32)
    for block in blocks:
        values = block[...].astype(jnp.float32)
        total = total + jnp.sum(values * values, axis=0, keepdims=True)
    scale = lax.rsqrt(total / features + epsilon)
    for kx in range(NX):
        for kz in range(NZ):
            x = lax.rem(place[0] + NX - kx, NX)
            z = lax.rem(place[1] + NZ - kz, NZ)
            rows = pl.ds(pl.multiple_of((x * NZ + z) * width, width), width)
            values = blocks[kx * NZ + kz][...].astype(jnp.float32)
            normed[rows, :] = (values * scale * gain[rows, :]).astype(jnp.bfloat16)
    kv_out[...] = jnp.dot(
        wkv_t[...], normed[...], preferred_element_type=jnp.float32
    ).astype(jnp.bfloat16)
    queries = lax.dot_general(
        normed[...], wq[...], (((0,), (0,)), ((), ())), preferred_element_type=jnp.float32
    )
    for head in range(HEADS):
        values = queries[:, head * HD : (head + 1) * HD]
        mean_square = jnp.mean(values * values, axis=1, keepdims=True)
        values = values * lax.rsqrt(mean_square + epsilon) * q_gain[...]
        turned = values * cosine[...] + pltpu.roll(values, HD // 2, 1) * sine[...]
        q_out[head] = turned.astype(jnp.bfloat16)


def project(place, blocks, gain, wq, wkv_t, q_gain, cosine, sine):
    vmem = pl.BlockSpec(memory_space=pltpu.VMEM)
    return pl.pallas_call(
        project_kernel,
        in_specs=[pl.BlockSpec(memory_space=pltpu.SMEM)] + [vmem] * (len(blocks) + 6),
        out_specs=[vmem, vmem],
        out_shape=[
            jax.ShapeDtypeStruct((HEADS, ROWS, HD), jnp.bfloat16),
            jax.ShapeDtypeStruct((wkv_t.shape[0], ROWS), jnp.bfloat16),
        ],
        scratch_shapes=[pltpu.VMEM((wq.shape[0], ROWS), jnp.bfloat16)],
        compiler_params=pltpu.CompilerParams(vmem_limit_bytes=VMEM),
        cost_estimate=pl.CostEstimate(
            flops=2 * ROWS * 5120 * 640, bytes_accessed=12_000_000, transcendentals=0
        ),
    )(place, *blocks, gain, wq, wkv_t, q_gain, cosine, sine)


def fold(q, keys, values, top, total, keep):
    scores = jnp.dot(q, keys, preferred_element_type=jnp.float32) * (LOG2E / math.sqrt(HD))
    if keep is not None:
        scores = jnp.where(keep, scores, -1e30)
    new_top = jnp.maximum(top, jnp.max(scores, axis=1, keepdims=True))
    factor = jnp.exp2(top - new_top)
    weights = jnp.exp2(scores - new_top[:, :1]).astype(jnp.bfloat16)
    added = lax.dot_general(
        weights, values, (((1,), (1,)), ((), ())), preferred_element_type=jnp.float32
    )
    return new_top, total * jnp.concatenate([factor, factor], axis=1) + added


def with_ones(values):
    return jnp.concatenate([values, jnp.ones_like(values)], axis=0)


def cache_kernel(offset, q, kv, top_out, total_out):
    step = pl.program_id(0)
    count = kv.shape[0]
    width = kv.shape[2]

    @pl.when(step == 0)
    def _():
        top_out[...] = jnp.full(top_out.shape, -1e30, jnp.float32)
        total_out[...] = jnp.zeros(total_out.shape, jnp.float32)

    def run(masked):
        keys = jnp.concatenate([kv[i, :HD, :] for i in range(count)], axis=1)
        values = with_ones(jnp.concatenate([kv[i, HD:, :] for i in range(count)], axis=1))
        keep = None
        if masked:
            slot = lax.broadcasted_iota(jnp.int32, (ROWS, count * width), 1)
            keep = slot + step * (count * width) < offset[0]
        for head in range(HEADS):
            top_out[head], total_out[head] = fold(
                q[head], keys, values, top_out[head], total_out[head], keep
            )

    full = (step + 1) * (count * width) <= offset[0]
    pl.when(full)(lambda: run(False))
    pl.when(jnp.logical_not(full))(lambda: run(True))


def attend_cache(offset, q, kv, per_step):
    steps = kv.shape[0] // per_step
    whole = lambda i: (0, 0, 0)
    return pl.pallas_call(
        cache_kernel,
        grid=(steps,),
        in_specs=[
            pl.BlockSpec(memory_space=pltpu.SMEM),
            pl.BlockSpec(q.shape, whole),
            pl.BlockSpec((per_step,) + kv.shape[1:], lambda i: (i, 0, 0)),
        ],
        out_specs=[
            pl.BlockSpec((HEADS, ROWS, HD), whole),
            pl.BlockSpec((HEADS, ROWS, 2 * HD), whole),
        ],
        out_shape=[
            jax.ShapeDtypeStruct((HEADS, ROWS, HD), jnp.float32),
            jax.ShapeDtypeStruct((HEADS, ROWS, 2 * HD), jnp.float32),
        ],
        compiler_params=pltpu.CompilerParams(vmem_limit_bytes=VMEM),
        cost_estimate=pl.CostEstimate(
            flops=4 * HEADS * ROWS * HD * 8192, bytes_accessed=8_000_000, transcendentals=HEADS * ROWS * 8192
        ),
    )(offset, q, kv)


def span_kernel(place, q, kv, own, top_in, total_in, out, top_ref, total_ref):
    step = pl.program_id(0)
    count = kv.shape[0]
    width = kv.shape[2]
    mine = place[0]

    @pl.when(step == 0)
    def _():
        top_ref[...] = top_in[...]
        total_ref[...] = total_in[...]

    def joined():
        keys = jnp.concatenate([kv[i, :HD, :] for i in range(count)], axis=1)
        values = with_ones(jnp.concatenate([kv[i, HD:, :] for i in range(count)], axis=1))
        return keys, values

    def run(masked):
        keys, values = joined()
        keep = None
        if masked:
            row = lax.broadcasted_iota(jnp.int32, (ROWS, count * width), 0)
            slot = lax.broadcasted_iota(jnp.int32, (ROWS, count * width), 1)
            keep = (row >= SPAN_ROWS) | (slot + step * (count * width) <= row + mine * SPAN_ROWS)
        for head in range(HEADS):
            top_ref[head], total_ref[head] = fold(
                q[head], keys, values, top_ref[head], total_ref[head], keep
            )

    def run_cand():
        keys, values = joined()
        for head in range(HEADS):
            top_ref[head, SPAN_ROWS:], total_ref[head, SPAN_ROWS:] = fold(
                q[head, SPAN_ROWS:], keys, values, top_ref[head, SPAN_ROWS:],
                total_ref[head, SPAN_ROWS:], None,
            )

    full = step * count + count - 1 < mine
    none = step * count > mine
    pl.when(full)(lambda: run(False))
    pl.when(none)(run_cand)
    pl.when(jnp.logical_not(full | none))(lambda: run(True))

    @pl.when(step == pl.num_programs(0) - 1)
    def _():
        values = with_ones(own[HD:, :])
        row = lax.broadcasted_iota(jnp.int32, (CAND_ROWS, CAND_ROWS), 0)
        slot = lax.broadcasted_iota(jnp.int32, (CAND_ROWS, CAND_ROWS), 1)
        for head in range(HEADS):
            _, total = fold(
                q[head, SPAN_ROWS:], own[:HD, :], values, top_ref[head, SPAN_ROWS:],
                total_ref[head, SPAN_ROWS:], slot <= row,
            )
            total = jnp.concatenate([total_ref[head, :SPAN_ROWS], total], axis=0)
            attended = total[:, :HD] / total[:, HD:]
            out[head * HD : (head + 1) * HD, :] = attended.T.astype(jnp.bfloat16)


def attend_span(place, q, kv, own, top, total, per_step):
    steps = kv.shape[0] // per_step
    whole = lambda i: (0, 0, 0)
    flat = lambda i: (0, 0)
    return pl.pallas_call(
        span_kernel,
        grid=(steps,),
        in_specs=[
            pl.BlockSpec(memory_space=pltpu.SMEM),
            pl.BlockSpec(q.shape, whole),
            pl.BlockSpec((per_step,) + kv.shape[1:], lambda i: (i, 0, 0)),
            pl.BlockSpec(own.shape, flat),
            pl.BlockSpec(top.shape, whole),
            pl.BlockSpec(total.shape, whole),
        ],
        out_specs=pl.BlockSpec((HEADS * HD, ROWS), flat),
        out_shape=jax.ShapeDtypeStruct((HEADS * HD, ROWS), jnp.bfloat16),
        scratch_shapes=[
            pltpu.VMEM(top.shape, jnp.float32),
            pltpu.VMEM(total.shape, jnp.float32),
        ],
        compiler_params=pltpu.CompilerParams(vmem_limit_bytes=VMEM),
        cost_estimate=pl.CostEstimate(
            flops=4 * HEADS * ROWS * HD * 4096, bytes_accessed=8_000_000, transcendentals=HEADS * ROWS * 4096
        ),
    )(place, q, kv, own, top, total)


def join_pair(mine, other, parity):
    half = mine.shape[0] // 2
    low = jnp.where(parity == 0, mine, other)
    high = jnp.where(parity == 0, other, mine)
    return jnp.concatenate([low[:half], high[:half], low[half:], high[half:]], axis=0)


def per_device(
    span_x, cand_x, cand_len, offset, norm_gain, wq, wk, wv, q_gain, k_gain, wo, cache_k, cache_v
):
    head = lax.axis_index("head")
    seq = lax.axis_index("seq").astype(jnp.int32)
    at_x, at_z = head // NZ, head % NZ
    parity = head % 2
    width = span_x.shape[1]
    half = HD // 2

    own_x = jnp.concatenate([span_x.T, cand_x[0].T], axis=1)
    blocks = [[None] * NZ for _ in range(NX)]
    blocks[0][0] = own_x
    for kz in (2, 1, 3):
        blocks[0][kz] = move_z(own_x, kz)
    for kx in (2, 1, 3):
        blocks[kx][0] = move_x(own_x, kx)
    for kz in (1, 3):
        blocks[2][kz] = move_z(blocks[2][0], kz)
    for kz in (1, 3, 2):
        for kx in (1, 3, 2):
            if blocks[kx][kz] is None:
                blocks[kx][kz] = move_x(blocks[0][kz], kx)

    cache_half = jnp.concatenate([cache_k.T, cache_v.T], axis=0)
    cache_block = join_pair(cache_half, swap_pair(cache_half), parity)
    cache_all = lax.all_gather(cache_block, "seq")

    start = offset[0]
    span_positions = start + seq * SPAN_ROWS + jnp.arange(SPAN_ROWS, dtype=jnp.int32)
    cand_positions = start + SPAN_ROWS * lax.axis_size("seq") + jnp.arange(CAND_ROWS, dtype=jnp.int32)
    positions = jnp.concatenate([span_positions, cand_positions]).astype(jnp.float32)
    frequency = rope_base ** (-(jnp.arange(half, dtype=jnp.float32) * 2.0 / HD))
    angles = frequency[:, None] * positions[None, :]
    cosine, sine = jnp.cos(angles), jnp.sin(angles)
    q_cosine = jnp.concatenate([cosine, cosine], axis=0).T
    q_sine = jnp.concatenate([-sine, sine], axis=0).T

    place = jnp.stack([at_x, at_z]).astype(jnp.int32)
    wkv_t = jnp.concatenate([wk.T, wv.T], axis=0)
    q, kv_half = project(
        place, [b for row in blocks for b in row], norm_gain[:, None], wq, wkv_t,
        q_gain[None, :], q_cosine, q_sine,
    )

    kv_new = join_pair(kv_half, swap_pair(kv_half), parity)
    raw = kv_new[:HD].astype(jnp.float32)
    raw = raw * lax.rsqrt(jnp.mean(raw * raw, axis=0, keepdims=True) + epsilon) * k_gain[:, None]
    front, back = raw[:half], raw[half:]
    new_keys = jnp.concatenate(
        [front * cosine - back * sine, back * cosine + front * sine], axis=0
    ).astype(jnp.bfloat16)
    new_block = jnp.concatenate([new_keys, kv_new[HD:]], axis=0)
    span_all = lax.all_gather(new_block[:, :SPAN_ROWS], "seq")
    own_block = new_block[:, SPAN_ROWS:]

    top, total = attend_cache(offset, q, cache_all, 2)
    attended = attend_span(seq[None], q, span_all, own_block, top, total, 4)

    wo_t = wo.T
    quarter = NZ * width
    terms = []
    for kx in range(NX):
        rows = (at_x + kx) % NX * quarter
        part = lax.dynamic_slice(wo_t, (rows, 0), (quarter, wo.shape[0]))
        terms.append(
            jnp.dot(part, attended, preferred_element_type=jnp.float32).astype(jnp.bfloat16)
        )
    summed = terms[0].astype(jnp.float32)
    for kx in (2, 1, 3):
        summed = summed + move_x(terms[kx], kx).astype(jnp.float32)
    summed = summed.astype(jnp.bfloat16)
    pieces = [
        lax.dynamic_slice(summed, ((at_z + kz) % NZ * width, 0), (width, ROWS))
        for kz in range(NZ)
    ]
    result = pieces[0].astype(jnp.float32)
    for kz in (2, 1, 3):
        result = result + move_z(pieces[kz], kz).astype(jnp.float32)
    span_out = result[:, :SPAN_ROWS].astype(jnp.bfloat16).T
    valid = jnp.arange(CAND_ROWS, dtype=jnp.int32)[None, :] < cand_len[0]
    cand_out = jnp.where(valid, result[:, SPAN_ROWS:], 0.0).astype(jnp.bfloat16).T[None]
    return span_out, cand_out


def solution(mesh):
    in_specs = (
        P("seq", "head"),
        P("seq", None, "head"),
        P("seq"),
        P(),
        P(),
        P(None, "head"),
        P(None, "head"),
        P(None, "head"),
        P(),
        P(),
        P("head", None),
        P("seq", "head"),
        P("seq", "head"),
    )
    out_specs = (P("seq", "head"), P("seq", None, "head"))
    return jax.shard_map(
        per_device, mesh=mesh, in_specs=in_specs, out_specs=out_specs, check_vma=False
    )
```

time: 527 us -> 256 us (0.49)
  waiting for transfers between devices: 258 us -> 108 us
  other arithmetic: 94.6 us -> 7.83 us
  matrix products: 91.8 us -> 11.2 us
  Pallas kernels: 0 us -> 62.6 us
  starting transfers between devices: 2.26 us -> 40.6 us
  local copies, waits for them, and re-layouts: 38.6 us -> 5.5 us
  loops' own time: 21.7 us -> 0 us
    all_gather x3 -> x2, waiting for transfers between devices: 155 us -> 22.7 us  [the longest x1 22.7 us: per_device(): span_all = lax.all_gather(new_block[:, :SPAN_ROWS], 'seq')]
    reduce_scatter x1 -> x0, waiting for transfers between devices: 91.7 us -> none  [per_device(): lax.psum_scatter(terms.astype(jnp.bfloat16), 'head', scatter_dimension=1,...]
    dot_general x38 -> x4, matrix products: 91.8 us -> 11.2 us  [per_device(): jnp.dot(part, attended, preferred_element_type=jnp.float32)]
    ppermute x1 -> x23, waiting for transfers between devices: 9.77 us -> 85 us  [the longest x13 38.3 us: move_x(): return lax.ppermute(block, 'head', route)]
    pallas_call x0 -> x3, Pallas kernels: none -> 62.6 us  [the longest x1 27.3 us: attend_cache(): pl.pallas_call(cache_kernel, grid=(steps,), in_specs=[pl.BlockSpec(memory...]
    reduce_sum x20 -> x1, other arithmetic: 62.2 us -> 0.04 us  [per_device(): jnp.mean(raw * raw, axis=0, keepdims=True) + epsilon]
    ppermute x1 -> x23, starting transfers between devices: 2.1 us -> 40.5 us  [the longest x8 23.5 us: move_z(): return lax.ppermute(block, 'head', route)]
    another operation x1 -> x0, loops' own time: 21.7 us -> none  [attend_source(): lax.scan(fold_block, initial, (jnp.arange(blocks.shape[0], dtype=jnp.int3...]
  transfers between devices with their start and end apart: 5 -> 25, of which waited for: 5 -> 14; matrix products, arithmetic and copies ran while one was open for 2% -> 6% of each run, Pallas kernels for 0% -> 15%
where the time goes in v1:
time: 256 us; the launch traced here: 252 us
  waiting for transfers between devices  108 us (42%)
  Pallas kernels  62.6 us (24%)
  starting transfers between devices  40.6 us (16%)
  between operations  16.1 us (6%)
  matrix products  11.2 us (4%)
  other arithmetic  7.83 us (3%)
  local copies, waits for them, and re-layouts  5.5 us (2%)
    ppermute x13, waiting for transfers between devices, move_x(): return lax.ppermute(block, 'head', route)  38.3 us
    ppermute x8, waiting for transfers between devices, move_z(): return lax.ppermute(block, 'head', route)  36 us
    pallas_call x1, Pallas kernels, attend_cache(): pl.pallas_call(cache_kernel, grid=(steps,), in_specs=[pl.BlockSpec(memory...  27.3 us
    pallas_call x1, Pallas kernels, attend_span(): pl.pallas_call(span_kernel, grid=(steps,), in_specs=[pl.BlockSpec(memory_...  24.5 us
    ppermute x8, starting transfers between devices, move_z(): return lax.ppermute(block, 'head', route)  23.5 us
    all_gather x1, waiting for transfers between devices, per_device(): span_all = lax.all_gather(new_block[:, :SPAN_ROWS], 'seq')  22.7 us
    ppermute x13, starting transfers between devices, move_x(): return lax.ppermute(block, 'head', route)  13.8 us
    dot_general x4, matrix products, per_device(): jnp.dot(part, attended, preferred_element_type=jnp.float32)  11.2 us
  transfers between devices with their start and end apart: 25, of which 14 were waited for; matrix products, arithmetic and copies ran while one was open for 6% of the time, Pallas kernels for 15%

profile of v1, /device:TPU:31, one launch (start us, length us, event | category | flops | bytes accessed | tf_op | source)
XLA Modules:
  0.0 251.5 jit_solution(12459598107001332147)
XLA Ops:
  7.2 1.0 pad_maximum_fusion.4
  8.2 3.1 %collective-permute-start.16 = (bf16[128,512]{1,0:T(8,128)(2,1)S(1)}, bf16[128,512]{1,0:T(8,128)(2,1)S(1)}, u32[]{:S(2)}, u32[]{:S(2)}) collective-permute-start(bf16[128,512]{1,0:T(8,128)(2,1)S(1)} %pad_maximum_fusion.4), channel_id=1, source_target_pairs={{0,1},{1,0},{2,3},{3,2},{4,5},{5,4},{6,7},{7,6},{8,9},{9,8},{10,11... | collective-permute-start | bytes 393224 | tf_op jit(solution)/shard_map/ppermute | solution.py:41
  11.3 6.0 %collective-permute-done.16 = bf16[128,512]{1,0:T(8,128)(2,1)S(1)} collective-permute-done((bf16[128,512]{1,0:T(8,128)(2,1)S(1)}, bf16[128,512]{1,0:T(8,128)(2,1)S(1)}, u32[]{:S(2)}, u32[]{:S(2)}) %collective-permute-start.16) | collective-permute-done | bytes 131104 | tf_op jit(solution)/shard_map/ppermute | solution.py:41
  17.4 0.9 broadcast_select_fusion.1
  18.3 0.7 pad_maximum_fusion.1
  19.2 6.6 %collective-permute-start.1 = (bf16[320,384]{1,0:T(8,128)(2,1)S(1)}, bf16[320,384]{1,0:T(8,128)(2,1)S(1)}, u32[]{:S(2)}, u32[]{:S(2)}) collective-permute-start(bf16[320,384]{1,0:T(8,128)(2,1)S(1)} %pad_maximum_fusion.2.refs_0_), channel_id=1, source_target_pairs={{0,2},{1,3},{2,0},{3,1},{4,6},{5,7},{6,4},{7,5},{8,10},{9,11},{10,... | collective-permute-start | bytes 737288 | tf_op jit(solution)/shard_map/ppermute | solution.py:37
  25.8 1.1 collective-permute-start.7
  26.9 3.6 %collective-permute-start.2 = (bf16[320,384]{1,0:T(8,128)(2,1)S(1)}, bf16[320,384]{1,0:T(8,128)(2,1)S(1)}, u32[]{:S(2)}, u32[]{:S(2)}) collective-permute-start(bf16[320,384]{1,0:T(8,128)(2,1)S(1)} %pad_maximum_fusion.2.refs_0_), channel_id=1, source_target_pairs={{0,3},{1,0},{2,1},{3,2},{4,7},{5,4},{6,5},{7,6},{8,11},{9,8},{10,9... | collective-permute-start | bytes 737288 | tf_op jit(solution)/shard_map/ppermute | solution.py:37
  30.5 1.2 pad_maximum_fusion.refs_18_
  32.3 1.8 collective-permute-done.1.refs_2_
  34.2 0.9 collective-permute-start.3
  35.6 11.4 %collective-permute-done.refs_1_ = bf16[320,384]{1,0:T(8,128)(2,1)S(1)} collective-permute-done((bf16[320,384]{1,0:T(8,128)(2,1)S(1)}, bf16[320,384]{1,0:T(8,128)(2,1)S(1)}, u32[]{:S(2)}, u32[]{:S(2)}) %collective-permute-start) | collective-permute-done | bytes 245792 | tf_op jit(solution)/shard_map/ppermute | solution.py:37
  47.0 0.5 collective-permute-start.5
  47.6 1.6 collective-permute-start.9
  49.2 1.7 collective-permute-start.10
  51.1 2.6 %collective-permute-start.4 = (bf16[320,384]{1,0:T(8,128)(2,1)S(1)}, bf16[320,384]{1,0:T(8,128)(2,1)}, u32[]{:S(2)}, u32[]{:S(2)}) collective-permute-start(bf16[320,384]{1,0:T(8,128)(2,1)S(1)} %collective-permute-done.refs_1_), channel_id=1, source_target_pairs={{0,4},{1,5},{2,6},{3,7},{4,8},{5,9},{6,10},{7,11},{8,12},{9,13},{1... | collective-permute-start | bytes 737288 | tf_op jit(solution)/shard_map/ppermute | solution.py:29
  54.1 3.1 %collective-permute-start.6 = (bf16[320,384]{1,0:T(8,128)(2,1)S(1)}, bf16[320,384]{1,0:T(8,128)(2,1)}, u32[]{:S(2)}, u32[]{:S(2)}) collective-permute-start(bf16[320,384]{1,0:T(8,128)(2,1)S(1)} %collective-permute-done.2.refs_3_), channel_id=1, source_target_pairs={{0,4},{1,5},{2,6},{3,7},{4,8},{5,9},{6,10},{7,11},{8,12},{9,13},{1... | collective-permute-start | bytes 737288 | tf_op jit(solution)/shard_map/ppermute | solution.py:29
  57.2 3.3 %collective-permute-start.8 = (bf16[320,384]{1,0:T(8,128)(2,1)S(1)}, bf16[320,384]{1,0:T(8,128)(2,1)}, u32[]{:S(2)}, u32[]{:S(2)}) collective-permute-start(bf16[320,384]{1,0:T(8,128)(2,1)S(1)} %collective-permute-done.7.refs_8_), channel_id=1, source_target_pairs={{0,1},{1,2},{2,3},{3,0},{4,5},{5,6},{6,7},{7,4},{8,9},{9,10},{10,1... | collective-permute-start | bytes 737288 | tf_op jit(solution)/shard_map/ppermute | solution.py:37
  61.0 0.8 copy.18.refs_20_
  61.8 0.8 copy.19.refs_21_
  62.6 2.4 copy.17.refs_16_
  65.1 0.6 pad_add_fusion.place
  65.7 1.1 collective-permute-done.6.refs_7_
  66.8 3.6 %collective-permute-done.8.refs_9_ = bf16[320,384]{1,0:T(8,128)(2,1)} collective-permute-done((bf16[320,384]{1,0:T(8,128)(2,1)S(1)}, bf16[320,384]{1,0:T(8,128)(2,1)}, u32[]{:S(2)}, u32[]{:S(2)}) %collective-permute-start.8) | collective-permute-done | bytes 245792 | tf_op jit(solution)/shard_map/ppermute | solution.py:37
  70.4 10.8 %shard_map.140 = (bf16[4,384,128]{2,1,0:T(8,128)(2,1)}, bf16[128,384]{1,0:T(8,128)(2,1)}) custom-call(s32[2]{0:T(128)} %pad_add_fusion.place, bf16[320,384]{1,0:T(8,128)(2,1)} %copy-done, bf16[320,384]{1,0:T(8,128)(2,1)} %copy-done.5, bf16[320,384]{1,0:T(8,128)(2,1)} %copy-done.3, bf16[320,384]{1,0:T(8,128)(2,1)} %copy-done.6, bf16[320,384]{1,0:T(8,128)(2,1)} %copy-done.8, ...), custom_call_target="tpu_custom_call" | custom-call | flops 2516582400 | bytes 12000000 | tf_op jit(solution)/shard_map/pallas_call | solution.py:77
  81.4 4.7 %collective-permute-done.15 = bf16[128,384]{1,0:T(8,128)(2,1)S(1)} collective-permute-done((bf16[128,384]{1,0:T(8,128)(2,1)}, bf16[128,384]{1,0:T(8,128)(2,1)S(1)}, u32[]{:S(2)}, u32[]{:S(2)}) %collective-permute-start.15) | collective-permute-done | bytes 98336 | tf_op jit(solution)/shard_map/ppermute | solution.py:41
  86.1 0.9 broadcast_select_fusion.3
  87.7 0.7 slice.67
  88.4 0.6 pad_maximum_fusion.6.own
  89.1 27.3 %shard_map.141 = (f32[4,384,128]{2,1,0:T(8,128)}, f32[4,384,256]{2,1,0:T(8,128)}) custom-call(s32[1]{0:T(128)} %copy.21.offset, bf16[4,384,128]{2,1,0:T(8,128)(2,1)} %get-tuple-element.6.q, bf16[16,256,512]{2,1,0:T(8,128)(2,1)} %bitcast.44), custom_call_target="tpu_custom_call" | custom-call | flops 6442450944 | bytes 8000000 | tf_op jit(solution)/shard_map/pallas_call | solution.py:140
  116.4 22.7 %all-gather.5.cloned.1.call-done = bf16[4096,256]{1,0:T(8,128)(2,1)} async-done(((bf16[256,256]{1,0:T(8,128)(2,1)}), bf16[4096,256]{1,0:T(8,128)(2,1)}) %all-gather.5.cloned.1.call-update) | async-done | bytes 2097168 | tf_op jit(solution)/shard_map/all_gather | solution.py:308
  139.0 24.5 %shard_map.142 = bf16[512,384]{1,0:T(8,128)(2,1)} custom-call(s32[1]{0:T(128)} %bitcast.place, bf16[4,384,128]{2,1,0:T(8,128)(2,1)} %get-tuple-element.6.q, bf16[16,256,256]{2,1,0:T(8,128)(2,1)} %bitcast.45, bf16[256,128]{1,0:T(8,128)(2,1)} %pad_maximum_fusion.6.own, f32[4,384,128]{2,1,0:T(8,128)} %get-tuple-element.8.top_in, ...), custom_call_target="tpu_custom_call" | custom-call | flops 3221225472 | bytes 8000000 | tf_op jit(solution)/shard_map/pallas_call | solution.py:224
  163.6 2.3 convolution_convert_fusion.2
  165.9 1.3 collective-permute-start.17
  167.1 3.2 %convolution_convert_fusion.1 = bf16[1280,384]{1,0:T(8,128)(2,1)} fusion(bf16[512,384]{1,0:T(8,128)(2,1)S(1)} %copy-done.17, bf16[512,5120]{1,0:T(8,128)(2,1)} %param.23, s32[]{:T(128)S(6)} %select_n.113), kind=kOutput, calls=%fused_computation.1 | convolution fusion | flops 503808000 | bytes 2686980 | tf_op jit(solution)/shard_map/dot_general | solution.py:321
  170.3 1.8 collective-permute-start.18
  172.1 3.2 %convolution_convert_fusion = bf16[1280,384]{1,0:T(8,128)(2,1)} fusion(bf16[512,384]{1,0:T(8,128)(2,1)S(1)} %copy-done.17, bf16[512,5120]{1,0:T(8,128)(2,1)} %param.23, s32[]{:T(128)S(6)} %select_n.115), kind=kOutput, calls=%fused_computation | convolution fusion | flops 503808000 | bytes 2686980 | tf_op jit(solution)/shard_map/dot_general | solution.py:321
  175.5 15.1 %collective-permute-done.17 = bf16[1280,384]{1,0:T(8,128)(2,1)S(1)} collective-permute-done((bf16[1280,384]{1,0:T(8,128)(2,1)S(1)}, bf16[1280,384]{1,0:T(8,128)(2,1)S(1)}, u32[]{:S(2)}, u32[]{:S(2)}) %collective-permute-start.17) | collective-permute-done | bytes 983072 | tf_op jit(solution)/shard_map/ppermute | solution.py:29
  190.6 19.0 %collective-permute-done.18 = bf16[1280,384]{1,0:T(8,128)(2,1)S(1)} collective-permute-done((bf16[1280,384]{1,0:T(8,128)(2,1)}, bf16[1280,384]{1,0:T(8,128)(2,1)S(1)}, u32[]{:S(2)}, u32[]{:S(2)}) %collective-permute-start.18) | collective-permute-done | bytes 983072 | tf_op jit(solution)/shard_map/ppermute | solution.py:29
  209.7 2.7 %collective-permute-done.19 = bf16[1280,384]{1,0:T(8,128)(2,1)} collective-permute-done((bf16[1280,384]{1,0:T(8,128)(2,1)}, bf16[1280,384]{1,0:T(8,128)(2,1)}, u32[]{:S(2)}, u32[]{:S(2)}) %collective-permute-start.19) | collective-permute-done | bytes 983072 | tf_op jit(solution)/shard_map/ppermute | solution.py:29
  212.3 2.6 %fusion.4 = bf16[1280,384]{1,0:T(8,128)(2,1)S(1)} fusion(bf16[512,384]{1,0:T(8,128)(2,1)S(1)} %copy-done.17, bf16[1280,384]{1,0:T(8,128)(2,1)} %collective-permute-done.19, bf16[1280,384]{1,0:T(8,128)(2,1)S(1)} %collective-permute-done.18, bf16[1280,384]{1,0:T(8,128)(2,1)S(1)} %collective-permute-done.17, bf16[512,5120]{1,0:T(8,128)(2,1)} %param.23, ...), kind=kOutput, calls=%fused_computation.8 | convolution fusion | flops 507740160 | bytes 5636100 | tf_op jit(solution)/shard_map/dot_general | solution.py:321
  215.0 4.7 %collective-permute-start.20 = (bf16[320,384]{1,0:T(8,128)(2,1)S(1)}, bf16[320,384]{1,0:T(8,128)(2,1)S(1)}, u32[]{:S(2)}, u32[]{:S(2)}) collective-permute-start(bf16[320,384]{1,0:T(8,128)(2,1)S(1)} %get-tuple-element.10), channel_id=1, source_target_pairs={{0,2},{1,3},{2,0},{3,1},{4,6},{5,7},{6,4},{7,5},{8,10},{9,11},{10,... | collective-permute-start | bytes 737288 | tf_op jit(solution)/shard_map/ppermute | solution.py:37
  220.1 3.1 %collective-permute-start.22 = (bf16[320,384]{1,0:T(8,128)(2,1)S(1)}, bf16[320,384]{1,0:T(8,128)(2,1)S(1)}, u32[]{:S(2)}, u32[]{:S(2)}) collective-permute-start(bf16[320,384]{1,0:T(8,128)(2,1)S(1)} %get-tuple-element.11), channel_id=1, source_target_pairs={{0,3},{1,0},{2,1},{3,2},{4,7},{5,4},{6,5},{7,6},{8,11},{9,8},{10,9... | collective-permute-start | bytes 737288 | tf_op jit(solution)/shard_map/ppermute | solution.py:37
  223.9 4.0 %collective-permute-done.20 = bf16[320,384]{1,0:T(8,128)(2,1)S(1)} collective-permute-done((bf16[320,384]{1,0:T(8,128)(2,1)S(1)}, bf16[320,384]{1,0:T(8,128)(2,1)S(1)}, u32[]{:S(2)}, u32[]{:S(2)}) %collective-permute-start.20) | collective-permute-done | bytes 245792 | tf_op jit(solution)/shard_map/ppermute | solution.py:37
  228.0 9.6 %collective-permute-done.21 = bf16[320,384]{1,0:T(8,128)(2,1)S(1)} collective-permute-done((bf16[320,384]{1,0:T(8,128)(2,1)S(1)}, bf16[320,384]{1,0:T(8,128)(2,1)S(1)}, u32[]{:S(2)}, u32[]{:S(2)}) %collective-permute-start.21) | collective-permute-done | bytes 245792 | tf_op jit(solution)/shard_map/ppermute | solution.py:37
  237.6 5.4 %collective-permute-done.22 = bf16[320,384]{1,0:T(8,128)(2,1)S(1)} collective-permute-done((bf16[320,384]{1,0:T(8,128)(2,1)S(1)}, bf16[320,384]{1,0:T(8,128)(2,1)S(1)}, u32[]{:S(2)}, u32[]{:S(2)}) %collective-permute-start.22) | collective-permute-done | bytes 245792 | tf_op jit(solution)/shard_map/ppermute | solution.py:37
  243.1 0.7 fusion.11
  243.8 0.7 fusion.20
  (78 shorter events, 3.3 us)
Async XLA Ops:
  7.2 11.9 %copy-start.13 = (bf16[256,320]{0,1:T(8,128)(2,1)S(1)}, bf16[256,320]{0,1:T(8,128)(2,1)}, u32[]{:S(2)}) copy-start(bf16[256,320]{0,1:T(8,128)(2,1)} %param.13) | copy-start | bytes 491524
  7.2 11.9 %copy-start.14 = (bf16[1,128,320]{1,2,0:T(8,128)(2,1)S(1)}, bf16[1,128,320]{1,2,0:T(8,128)(2,1)}, u32[]{:S(2)}) copy-start(bf16[1,128,320]{1,2,0:T(8,128)(2,1)} %param.14) | copy-start | bytes 245764
  7.2 23.3 %copy-start.2 = (bf16[5120,64]{0,1:T(8,128)(2,1)S(1)}, bf16[5120,64]{0,1:T(8,128)(2,1)}, u32[]{:S(2)}) copy-start(bf16[5120,64]{0,1:T(8,128)(2,1)} %param.19) | copy-start | bytes 1966084
  7.2 23.3 %copy-start.1 = (bf16[5120,64]{0,1:T(8,128)(2,1)S(1)}, bf16[5120,64]{0,1:T(8,128)(2,1)}, u32[]{:S(2)}) copy-start(bf16[5120,64]{0,1:T(8,128)(2,1)} %param.20) | copy-start | bytes 1966084
  7.2 81.9 %all-gather.7.cloned.1.call-start = ((), (), s32[]{:S(2)}) async-start(), calls=%async_computation.1 | async-start | bytes 4456448 | tf_op jit(solution)/shard_map/all_gather | solution.py:281
  8.2 9.1 %collective-permute-start.16 = (bf16[128,512]{1,0:T(8,128)(2,1)S(1)}, bf16[128,512]{1,0:T(8,128)(2,1)S(1)}, u32[]{:S(2)}, u32[]{:S(2)}) collective-permute-start(bf16[128,512]{1,0:T(8,128)(2,1)S(1)} %pad_maximum_fusion.4), channel_id=1, source_target_pairs={{0,1},{1,0},{2,3},{3,2},{4,5},{5,4},{6,7},{7,6},{8,9},{9,8},{10,11... | collective-permute-start | bytes 393224 | tf_op jit(solution)/shard_map/ppermute | solution.py:41
  19.0 120.0 %all-gather.5.cloned.1.call-start = ((), (), s32[]{:S(2)}) async-start(), calls=%async_computation | async-start | bytes 2228224 | tf_op jit(solution)/shard_map/all_gather | solution.py:308
  19.2 42.7 %copy-start = (bf16[320,384]{1,0:T(8,128)(2,1)}, bf16[320,384]{1,0:T(8,128)(2,1)S(1)}, u32[]{:S(2)}) copy-start(bf16[320,384]{1,0:T(8,128)(2,1)S(1)} %pad_maximum_fusion.2.refs_0_) | copy-start | bytes 737284
  19.2 15.0 %collective-permute-start.1 = (bf16[320,384]{1,0:T(8,128)(2,1)S(1)}, bf16[320,384]{1,0:T(8,128)(2,1)S(1)}, u32[]{:S(2)}, u32[]{:S(2)}) collective-permute-start(bf16[320,384]{1,0:T(8,128)(2,1)S(1)} %pad_maximum_fusion.2.refs_0_), channel_id=1, source_target_pairs={{0,2},{1,3},{2,0},{3,1},{4,6},{5,7},{6,4},{7,5},{8,10},{9,11},{10,... | collective-permute-start | bytes 737288 | tf_op jit(solution)/shard_map/ppermute | solution.py:37
  25.8 9.3 %collective-permute-start.7 = (bf16[320,384]{1,0:T(8,128)(2,1)S(1)}, bf16[320,384]{1,0:T(8,128)(2,1)S(1)}, u32[]{:S(2)}, u32[]{:S(2)}) collective-permute-start(bf16[320,384]{1,0:T(8,128)(2,1)S(1)} %pad_maximum_fusion.2.refs_0_), channel_id=1, source_target_pairs={{0,8},{1,9},{2,10},{3,11},{4,12},{5,13},{6,14},{7,15},{8,0},{9,1},... | collective-permute-start | bytes 737288 | tf_op jit(solution)/shard_map/ppermute | solution.py:29
  26.9 20.1 %collective-permute-start = (bf16[320,384]{1,0:T(8,128)(2,1)S(1)}, bf16[320,384]{1,0:T(8,128)(2,1)S(1)}, u32[]{:S(2)}, u32[]{:S(2)}) collective-permute-start(bf16[320,384]{1,0:T(8,128)(2,1)S(1)} %pad_maximum_fusion.2.refs_0_), channel_id=1, source_target_pairs={{0,1},{1,2},{2,3},{3,0},{4,5},{5,6},{6,7},{7,4},{8,9},{9,10},{10,1... | collective-permute-start | bytes 737288 | tf_op jit(solution)/shard_map/ppermute | solution.py:37
  26.9 20.6 %collective-permute-start.2 = (bf16[320,384]{1,0:T(8,128)(2,1)S(1)}, bf16[320,384]{1,0:T(8,128)(2,1)S(1)}, u32[]{:S(2)}, u32[]{:S(2)}) collective-permute-start(bf16[320,384]{1,0:T(8,128)(2,1)S(1)} %pad_maximum_fusion.2.refs_0_), channel_id=1, source_target_pairs={{0,3},{1,0},{2,1},{3,2},{4,7},{5,4},{6,5},{7,6},{8,11},{9,8},{10,9... | collective-permute-start | bytes 737288 | tf_op jit(solution)/shard_map/ppermute | solution.py:37
  30.5 18.7 %collective-permute-start.11 = (bf16[320,384]{1,0:T(8,128)(2,1)S(1)}, bf16[320,384]{1,0:T(8,128)(2,1)S(1)}, u32[]{:S(2)}, u32[]{:S(2)}) collective-permute-start(bf16[320,384]{1,0:T(8,128)(2,1)S(1)} %pad_maximum_fusion.2.refs_0_), channel_id=1, source_target_pairs={{0,12},{1,13},{2,14},{3,15},{4,0},{5,1},{6,2},{7,3},{8,4},{9,5},{1... | collective-permute-start | bytes 737288 | tf_op jit(solution)/shard_map/ppermute | solution.py:29
  30.5 32.1 %copy-start.15 = (f32[5120]{0:T(1024)S(1)}, f32[5120]{0:T(1024)}, u32[]{:S(2)}) copy-start(f32[5120]{0:T(1024)} %param.17) | copy-start | bytes 61444
  34.2 30.8 %copy-start.3 = (bf16[320,384]{1,0:T(8,128)(2,1)}, bf16[320,384]{1,0:T(8,128)(2,1)S(1)}, u32[]{:S(2)}) copy-start(bf16[320,384]{1,0:T(8,128)(2,1)S(1)} %collective-permute-done.1.refs_2_) | copy-start | bytes 737284
  34.2 16.8 %collective-permute-start.3 = (bf16[320,384]{1,0:T(8,128)(2,1)S(1)}, bf16[320,384]{1,0:T(8,128)(2,1)S(1)}, u32[]{:S(2)}, u32[]{:S(2)}) collective-permute-start(bf16[320,384]{1,0:T(8,128)(2,1)S(1)} %pad_maximum_fusion.2.refs_0_), channel_id=1, source_target_pairs={{0,4},{1,5},{2,6},{3,7},{4,8},{5,9},{6,10},{7,11},{8,12},{9,13},{1... | collective-permute-start | bytes 737288 | tf_op jit(solution)/shard_map/ppermute | solution.py:29
  35.1 29.9 %copy-start.4 = (bf16[320,384]{1,0:T(8,128)(2,1)}, bf16[320,384]{1,0:T(8,128)(2,1)S(1)}, u32[]{:S(2)}) copy-start(bf16[320,384]{1,0:T(8,128)(2,1)S(1)} %collective-permute-done.7.refs_8_) | copy-start | bytes 737284
  35.1 16.0 %collective-permute-start.13 = (bf16[320,384]{1,0:T(8,128)(2,1)S(1)}, bf16[320,384]{1,0:T(8,128)(2,1)S(1)}, u32[]{:S(2)}, u32[]{:S(2)}) collective-permute-start(bf16[320,384]{1,0:T(8,128)(2,1)S(1)} %collective-permute-done.1.refs_2_), channel_id=1, source_target_pairs={{0,12},{1,13},{2,14},{3,15},{4,0},{5,1},{6,2},{7,3},{8,4},{9,5},{1... | collective-permute-start | bytes 737288 | tf_op jit(solution)/shard_map/ppermute | solution.py:29
  47.0 18.0 %copy-start.5 = (bf16[320,384]{1,0:T(8,128)(2,1)}, bf16[320,384]{1,0:T(8,128)(2,1)S(1)}, u32[]{:S(2)}) copy-start(bf16[320,384]{1,0:T(8,128)(2,1)S(1)} %collective-permute-done.refs_1_) | copy-start | bytes 737284
  47.0 6.7 %collective-permute-start.5 = (bf16[320,384]{1,0:T(8,128)(2,1)S(1)}, bf16[320,384]{1,0:T(8,128)(2,1)S(1)}, u32[]{:S(2)}, u32[]{:S(2)}) collective-permute-start(bf16[320,384]{1,0:T(8,128)(2,1)S(1)} %collective-permute-done.1.refs_2_), channel_id=1, source_target_pairs={{0,4},{1,5},{2,6},{3,7},{4,8},{5,9},{6,10},{7,11},{8,12},{9,13},{1... | collective-permute-start | bytes 737288 | tf_op jit(solution)/shard_map/ppermute | solution.py:29
  47.6 17.4 %copy-start.6 = (bf16[320,384]{1,0:T(8,128)(2,1)}, bf16[320,384]{1,0:T(8,128)(2,1)S(1)}, u32[]{:S(2)}) copy-start(bf16[320,384]{1,0:T(8,128)(2,1)S(1)} %collective-permute-done.2.refs_3_) | copy-start | bytes 737284
  47.6 6.6 %collective-permute-start.9 = (bf16[320,384]{1,0:T(8,128)(2,1)S(1)}, bf16[320,384]{1,0:T(8,128)(2,1)S(1)}, u32[]{:S(2)}, u32[]{:S(2)}) collective-permute-start(bf16[320,384]{1,0:T(8,128)(2,1)S(1)} %collective-permute-done.1.refs_2_), channel_id=1, source_target_pairs={{0,8},{1,9},{2,10},{3,11},{4,12},{5,13},{6,14},{7,15},{8,0},{9,1},... | collective-permute-start | bytes 737288 | tf_op jit(solution)/shard_map/ppermute | solution.py:29
  49.2 15.8 %copy-start.7 = (bf16[320,384]{1,0:T(8,128)(2,1)}, bf16[320,384]{1,0:T(8,128)(2,1)S(1)}, u32[]{:S(2)}) copy-start(bf16[320,384]{1,0:T(8,128)(2,1)S(1)} %collective-permute-done.11.refs_12_) | copy-start | bytes 737284
  49.2 8.0 %collective-permute-start.10 = (bf16[320,384]{1,0:T(8,128)(2,1)S(1)}, bf16[320,384]{1,0:T(8,128)(2,1)S(1)}, u32[]{:S(2)}, u32[]{:S(2)}) collective-permute-start(bf16[320,384]{1,0:T(8,128)(2,1)S(1)} %collective-permute-done.7.refs_8_), channel_id=1, source_target_pairs={{0,3},{1,0},{2,1},{3,2},{4,7},{5,4},{6,5},{7,6},{8,11},{9,8},{10,9... | collective-permute-start | bytes 737288 | tf_op jit(solution)/shard_map/ppermute | solution.py:37
  51.0 14.1 %copy-start.8 = (bf16[320,384]{1,0:T(8,128)(2,1)}, bf16[320,384]{1,0:T(8,128)(2,1)S(1)}, u32[]{:S(2)}) copy-start(bf16[320,384]{1,0:T(8,128)(2,1)S(1)} %collective-permute-done.3.refs_4_) | copy-start | bytes 737284
  51.0 14.7 %collective-permute-start.12 = (bf16[320,384]{1,0:T(8,128)(2,1)S(1)}, bf16[320,384]{1,0:T(8,128)(2,1)}, u32[]{:S(2)}, u32[]{:S(2)}) collective-permute-start(bf16[320,384]{1,0:T(8,128)(2,1)S(1)} %collective-permute-done.refs_1_), channel_id=1, source_target_pairs={{0,12},{1,13},{2,14},{3,15},{4,0},{5,1},{6,2},{7,3},{8,4},{9,5},{1... | collective-permute-start | bytes 737288 | tf_op jit(solution)/shard_map/ppermute | solution.py:29
  51.1 13.9 %copy-start.9 = (bf16[320,384]{1,0:T(8,128)(2,1)}, bf16[320,384]{1,0:T(8,128)(2,1)S(1)}, u32[]{:S(2)}) copy-start(bf16[320,384]{1,0:T(8,128)(2,1)S(1)} %collective-permute-done.13.refs_14_) | copy-start | bytes 737284
  51.1 14.6 %collective-permute-start.4 = (bf16[320,384]{1,0:T(8,128)(2,1)S(1)}, bf16[320,384]{1,0:T(8,128)(2,1)}, u32[]{:S(2)}, u32[]{:S(2)}) collective-permute-start(bf16[320,384]{1,0:T(8,128)(2,1)S(1)} %collective-permute-done.refs_1_), channel_id=1, source_target_pairs={{0,4},{1,5},{2,6},{3,7},{4,8},{5,9},{6,10},{7,11},{8,12},{9,13},{1... | collective-permute-start | bytes 737288 | tf_op jit(solution)/shard_map/ppermute | solution.py:29
  53.7 11.3 %copy-start.10 = (bf16[320,384]{1,0:T(8,128)(2,1)}, bf16[320,384]{1,0:T(8,128)(2,1)S(1)}, u32[]{:S(2)}) copy-start(bf16[320,384]{1,0:T(8,128)(2,1)S(1)} %collective-permute-done.5.refs_6_) | copy-start | bytes 737284
  53.7 11.9 %collective-permute-start.14 = (bf16[320,384]{1,0:T(8,128)(2,1)S(1)}, bf16[320,384]{1,0:T(8,128)(2,1)}, u32[]{:S(2)}, u32[]{:S(2)}) collective-permute-start(bf16[320,384]{1,0:T(8,128)(2,1)S(1)} %collective-permute-done.2.refs_3_), channel_id=1, source_target_pairs={{0,12},{1,13},{2,14},{3,15},{4,0},{5,1},{6,2},{7,3},{8,4},{9,5},{1... | collective-permute-start | bytes 737288 | tf_op jit(solution)/shard_map/ppermute | solution.py:29
  54.1 10.9 %copy-start.11 = (bf16[320,384]{1,0:T(8,128)(2,1)}, bf16[320,384]{1,0:T(8,128)(2,1)S(1)}, u32[]{:S(2)}) copy-start(bf16[320,384]{1,0:T(8,128)(2,1)S(1)} %collective-permute-done.9.refs_10_) | copy-start | bytes 737284
  54.1 12.7 %collective-permute-start.6 = (bf16[320,384]{1,0:T(8,128)(2,1)S(1)}, bf16[320,384]{1,0:T(8,128)(2,1)}, u32[]{:S(2)}, u32[]{:S(2)}) collective-permute-start(bf16[320,384]{1,0:T(8,128)(2,1)S(1)} %collective-permute-done.2.refs_3_), channel_id=1, source_target_pairs={{0,4},{1,5},{2,6},{3,7},{4,8},{5,9},{6,10},{7,11},{8,12},{9,13},{1... | collective-permute-start | bytes 737288 | tf_op jit(solution)/shard_map/ppermute | solution.py:29
  57.2 7.8 %copy-start.12 = (bf16[320,384]{1,0:T(8,128)(2,1)}, bf16[320,384]{1,0:T(8,128)(2,1)S(1)}, u32[]{:S(2)}) copy-start(bf16[320,384]{1,0:T(8,128)(2,1)S(1)} %collective-permute-done.10.refs_11_) | copy-start | bytes 737284
  57.2 13.2 %collective-permute-start.8 = (bf16[320,384]{1,0:T(8,128)(2,1)S(1)}, bf16[320,384]{1,0:T(8,128)(2,1)}, u32[]{:S(2)}, u32[]{:S(2)}) collective-permute-start(bf16[320,384]{1,0:T(8,128)(2,1)S(1)} %collective-permute-done.7.refs_8_), channel_id=1, source_target_pairs={{0,1},{1,2},{2,3},{3,0},{4,5},{5,6},{6,7},{7,4},{8,9},{9,10},{10,1... | collective-permute-start | bytes 737288 | tf_op jit(solution)/shard_map/ppermute | solution.py:37
  70.4 16.6 %copy-start.16 = (f32[128]{0:T(128)S(1)}, f32[128]{0:T(128)}, u32[]{:S(2)}) copy-start(f32[128]{0:T(128)} %param.22) | copy-start | bytes 1540
  81.3 4.8 %collective-permute-start.15 = (bf16[128,384]{1,0:T(8,128)(2,1)}, bf16[128,384]{1,0:T(8,128)(2,1)S(1)}, u32[]{:S(2)}, u32[]{:S(2)}) collective-permute-start(bf16[128,384]{1,0:T(8,128)(2,1)} %get-tuple-element.7), channel_id=1, source_target_pairs={{0,1},{1,0},{2,3},{3,2},{4,5},{5,4},{6,7},{7,6},{8,9},{9,8},{10,11... | collective-permute-start | bytes 294920 | tf_op jit(solution)/shard_map/ppermute | solution.py:41
  163.6 3.6 %copy-start.17 = (bf16[512,384]{1,0:T(8,128)(2,1)S(1)}, bf16[512,384]{1,0:T(8,128)(2,1)}, u32[]{:S(2)}) copy-start(bf16[512,384]{1,0:T(8,128)(2,1)} %shard_map.142) | copy-start | bytes 1179652
  165.9 24.7 %collective-permute-start.17 = (bf16[1280,384]{1,0:T(8,128)(2,1)S(1)}, bf16[1280,384]{1,0:T(8,128)(2,1)S(1)}, u32[]{:S(2)}, u32[]{:S(2)}) collective-permute-start(bf16[1280,384]{1,0:T(8,128)(2,1)S(1)} %convolution_convert_fusion.2), channel_id=1, source_target_pairs={{0,8},{1,9},{2,10},{3,11},{4,12},{5,13},{6,14},{7,15},{8,0},{9,1},... | collective-permute-start | bytes 2949128 | tf_op jit(solution)/shard_map/ppermute | solution.py:29
  170.3 39.4 %collective-permute-start.18 = (bf16[1280,384]{1,0:T(8,128)(2,1)}, bf16[1280,384]{1,0:T(8,128)(2,1)S(1)}, u32[]{:S(2)}, u32[]{:S(2)}) collective-permute-start(bf16[1280,384]{1,0:T(8,128)(2,1)} %convolution_convert_fusion.1), channel_id=1, source_target_pairs={{0,4},{1,5},{2,6},{3,7},{4,8},{5,9},{6,10},{7,11},{8,12},{9,13},{1... | collective-permute-start | bytes 2949128 | tf_op jit(solution)/shard_map/ppermute | solution.py:29
  175.2 37.1 %collective-permute-start.19 = (bf16[1280,384]{1,0:T(8,128)(2,1)}, bf16[1280,384]{1,0:T(8,128)(2,1)}, u32[]{:S(2)}, u32[]{:S(2)}) collective-permute-start(bf16[1280,384]{1,0:T(8,128)(2,1)} %convolution_convert_fusion), channel_id=1, source_target_pairs={{0,12},{1,13},{2,14},{3,15},{4,0},{5,1},{6,2},{7,3},{8,4},{9,5},{1... | collective-permute-start | bytes 2949128 | tf_op jit(solution)/shard_map/ppermute | solution.py:29
  215.0 12.9 %collective-permute-start.20 = (bf16[320,384]{1,0:T(8,128)(2,1)S(1)}, bf16[320,384]{1,0:T(8,128)(2,1)S(1)}, u32[]{:S(2)}, u32[]{:S(2)}) collective-permute-start(bf16[320,384]{1,0:T(8,128)(2,1)S(1)} %get-tuple-element.10), channel_id=1, source_target_pairs={{0,2},{1,3},{2,0},{3,1},{4,6},{5,7},{6,4},{7,5},{8,10},{9,11},{10,... | collective-permute-start | bytes 737288 | tf_op jit(solution)/shard_map/ppermute | solution.py:37
  219.7 17.9 %collective-permute-start.21 = (bf16[320,384]{1,0:T(8,128)(2,1)S(1)}, bf16[320,384]{1,0:T(8,128)(2,1)S(1)}, u32[]{:S(2)}, u32[]{:S(2)}) collective-permute-start(bf16[320,384]{1,0:T(8,128)(2,1)S(1)} %get-tuple-element.12), channel_id=1, source_target_pairs={{0,1},{1,2},{2,3},{3,0},{4,5},{5,6},{6,7},{7,4},{8,9},{9,10},{10,1... | collective-permute-start | bytes 737288 | tf_op jit(solution)/shard_map/ppermute | solution.py:37
  220.1 22.9 %collective-permute-start.22 = (bf16[320,384]{1,0:T(8,128)(2,1)S(1)}, bf16[320,384]{1,0:T(8,128)(2,1)S(1)}, u32[]{:S(2)}, u32[]{:S(2)}) collective-permute-start(bf16[320,384]{1,0:T(8,128)(2,1)S(1)} %get-tuple-element.11), channel_id=1, source_target_pairs={{0,3},{1,0},{2,1},{3,2},{4,7},{5,4},{6,5},{7,6},{8,11},{9,8},{10,9... | collective-permute-start | bytes 737288 | tf_op jit(solution)/shard_map/ppermute | solution.py:37
Sparse Core Ops, SparseCore 0:
  19.2 61.2 all-gather.6
  88.5 50.5 all-gather.4
